TPU v7x, 32 devices: a whole 2x2x4 slice. The times are simulated.
32 devices in a mesh: grp: 2 (over y), gx: 4 (over z), gy: 2 (over x), wa: 2 (over core).
Axes of the slice: x: 2, y: 2, z: 4, core: 2. Of those that a mesh axis runs over, the one named last changes fastest.
Arguments:
- fine_iterate: float32 [128, 128, 1024], P(('grp', 'gx'), 'gy', 'wa'), parts along dimension 0, may hold values from -6 to 6
- fine_rhs: float32 [128, 128, 1024], P(('grp', 'gx'), 'gy', 'wa'), parts along dimension 0, may hold values from -6 to 6
- fine_ids: int32 [128, 128, 1024], P(('grp', 'gx'), 'gy', 'wa'), parts along dimension 0, may hold values from 0 to 7
- level_iterate: float32 [64, 64, 512], P(('grp', 'gx')), parts along dimension 0, may hold values from -6 to 6
- level_rhs: float32 [64, 64, 512], P(('grp', 'gx')), parts along dimension 0, may hold values from -6 to 6
- level_ids: int32 [64, 64, 512], P(('grp', 'gx')), parts along dimension 0, may hold values from 0 to 7
- coarse_update: float32 [32, 32, 256], P(('grp', 'gx')), parts along dimension 0, may hold values from -6 to 6
- conductivity: float32 [8], replicated, may hold values from 0.1 to 10
Outputs:
- smoothed: float32 [128, 128, 1024], P(('grp', 'gx'), 'gy', 'wa'), parts along dimension 0
There are 2 independent parts, one for each index of `grp`. A program takes and returns all parts, laid end to end along the dimension named above; an argument that names none is the same for every part. Nothing has to cross between parts.
All inputs are finite; a program needn't handle non-finite values.
Results may differ from a plain program's by a relative error of at most 0.00012.
Values sent between devices are 32-bit elements; how exact they have to be, the bound alone decides.
A program may use at most 128 MiB of HBM per device.

v0:
```python
import jax
import jax.numpy as jnp
from jax import lax
from jax.sharding import PartitionSpec as P


def extended(block, sides, width):
    for axis, dim in sides:
        count = lax.axis_size(axis)
        forward = [(i, i + 1) for i in range(count - 1)]
        backward = [(target, source) for source, target in forward]
        low = lax.ppermute(
            lax.slice_in_dim(block, block.shape[dim] - width, None, axis=dim), axis, forward
        )
        high = lax.ppermute(lax.slice_in_dim(block, 0, width, axis=dim), axis, backward)
        block = jnp.concatenate([low, block, high], axis=dim)
    return block


def lookup(ids, table):
    kappa = jnp.zeros(ids.shape, jnp.float32)
    for material in range(table.shape[0]):
        kappa = jnp.where(ids == material, table[material], kappa)
    return kappa


def neighbours(ext):
    return [
        ext[:-2, 1:-1, 1:-1],
        ext[2:, 1:-1, 1:-1],
        ext[1:-1, :-2, 1:-1],
        ext[1:-1, 2:, 1:-1],
        ext[1:-1, 1:-1, :-2],
        ext[1:-1, 1:-1, 2:],
    ]


def face_weights(kappa_ext):
    centre = kappa_ext[1:-1, 1:-1, 1:-1]
    weights = [0.5 * (centre + other) for other in neighbours(kappa_ext)]
    total = weights[0]
    for extra in weights[1:]:
        total = total + extra
    return (weights, total)


def scaled_residual(field_ext, rhs, weights, total):
    image = total * field_ext[1:-1, 1:-1, 1:-1]
    for weight, other in zip(weights, neighbours(field_ext)):
        image = image - weight * other
    return (rhs - image) / total


def smooth(first_ext, rhs, weights, total, extend):
    step_one = scaled_residual(first_ext, rhs, weights, total) / 1.2
    field = first_ext[1:-1, 1:-1, 1:-1] + step_one
    step_two = 2.0 / 7.0 * step_one + 15.0 / 14.0 * scaled_residual(
        extend(field), rhs, weights, total
    )
    return field + step_two


def spread_matrix(coarse_len, rim):
    fine_len = 2 * (coarse_len - 2) + 2 * rim
    cols = jnp.arange(fine_len, dtype=jnp.int32) - rim
    base = cols // 2
    parity = cols - 2 * base
    rowsix = jnp.arange(coarse_len, dtype=jnp.int32)[:, None]
    main = (rowsix == base[None, :] + 1).astype(jnp.float32)
    side = (rowsix == base[None, :] + 2 * parity[None, :]).astype(jnp.float32)
    return 0.75 * main + 0.25 * side


def prolong_axis(coarse, axis):
    count = coarse.shape[axis] - 2
    lower = lax.slice_in_dim(coarse, 0, count, axis=axis)
    middle = lax.slice_in_dim(coarse, 1, count + 1, axis=axis)
    upper = lax.slice_in_dim(coarse, 2, count + 2, axis=axis)
    even = 0.75 * middle + 0.25 * lower
    odd = 0.75 * middle + 0.25 * upper
    shape = list(coarse.shape)
    shape[axis] = 2 * count
    fine = jnp.stack([even, odd], axis=axis + 1).reshape(shape)
    return fine


def prolong(coarse, rim):
    field = prolong_axis(coarse, 0)
    field = prolong_axis(field, 1)
    matrix = spread_matrix(field.shape[2], rim)
    flat = field.reshape(-1, field.shape[2])
    out = jnp.dot(flat, matrix, precision=lax.Precision.HIGHEST, preferred_element_type=jnp.float32)
    return out.reshape(field.shape[0], field.shape[1], matrix.shape[1])


def slab_rim(field):
    grown = extended(field, (("gx", 0),), 1)
    return jnp.pad(grown, ((0, 0), (1, 1), (1, 1)))


def pencil_rim(field):
    return extended(field, (("gx", 0), ("gy", 1), ("wa", 2)), 1)


def window(field, row_start, row_len, col_start, col_len):
    part = lax.dynamic_slice_in_dim(field, row_start, row_len, 1)
    return lax.dynamic_slice_in_dim(part, col_start, col_len, 2)


def per_device(
    fine_iterate,
    fine_rhs,
    fine_ids,
    level_iterate,
    level_rhs,
    level_ids,
    coarse_update,
    conductivity,
):
    depth, rows, cols = fine_iterate.shape
    half_rows = rows // 2
    half_cols = cols // 2
    row_block = lax.axis_index("gy")
    col_block = lax.axis_index("wa")
    coarse_ext = slab_rim(coarse_update)
    level_kappa = lookup(level_ids, conductivity)
    start = level_iterate + prolong(coarse_ext, 0)
    weights, total = face_weights(slab_rim(level_kappa))
    settled = smooth(slab_rim(start), level_rhs, weights, total, slab_rim)
    settled_ext = slab_rim(settled)
    window_ext = window(
        settled_ext, row_block * half_rows, half_rows + 2, col_block * half_cols, half_cols + 2
    )
    fine_kappa = lookup(fine_ids, conductivity)
    fine_weights, fine_total = face_weights(pencil_rim(fine_kappa))
    first_ext = pencil_rim(fine_iterate + prolong(window_ext, 0))
    return smooth(first_ext, fine_rhs, fine_weights, fine_total, pencil_rim)


def solution(mesh):
    return jax.shard_map(
        per_device,
        mesh=mesh,
        in_specs=(
            P(("grp", "gx"), "gy", "wa"),
            P(("grp", "gx"), "gy", "wa"),
            P(("grp", "gx"), "gy", "wa"),
            P(("grp", "gx"), None, None),
            P(("grp", "gx"), None, None),
            P(("grp", "gx"), None, None),
            P(("grp", "gx"), None, None),
            P(),
        ),
        out_specs=P(("grp", "gx"), "gy", "wa"),
        check_vma=False,
    )
```

profile of v0, /device:TPU:0, one launch (start us, length us, event | category | flops | bytes accessed | tf_op | source)
XLA Modules:
  0.0 207.0 jit_solution(2606282581427129102)
XLA Ops:
  0.9 4.9 %collective-permute-start = (f32[1,32,256]{2,1,0:T(8,128)S(1)}, f32[1,32,256]{2,1,0:T(8,128)S(1)}, u32[]{:S(2)}, u32[]{:S(2)}) collective-permute-start(f32[1,32,256]{2,1,0:T(8,128)S(1)} %get-tuple-element.43), channel_id=1, source_target_pairs={{0,4},{4,8},{8,12},{1,5},{5,9},{9,13},{2,6},{6,10},{10,14},{3,7},{... | collective-permute-start | bytes 98312 | tf_op jit(solution)/shard_map/ppermute | solution.py:12
  8.8 6.7 %select_select_fusion.1 = f32[8,64,512]{2,1,0:T(8,128)S(1)} fusion(s32[8,64,512]{2,1,0:T(8,128)} %param.13, f32[]{:T(128)} %bitcast.12, f32[]{:T(128)} %bitcast.11, f32[]{:T(128)} %bitcast.10, f32[]{:T(128)} %bitcast.9, f32[]{:T(128)} %bitcast.8, f32[]{:T(128)} %bitcast.7, f32[]{:T(128)} %bitcast.6, f32[]{:T(128)} %bitcast.5), kind=kLoop, calls=%fused_computation.169 | loop fusion | flops 4194304 | bytes 2097184 | tf_op jit(solution)/shard_map/jit(_where)/select_n | solution.py:23
  15.5 4.6 %collective-permute-start.2 = (f32[1,64,512]{2,1,0:T(8,128)S(1)}, f32[1,64,512]{2,1,0:T(8,128)S(1)}, u32[]{:S(2)}, u32[]{:S(2)}) collective-permute-start(f32[1,64,512]{2,1,0:T(8,128)S(1)} %get-tuple-element.31), channel_id=1, source_target_pairs={{0,4},{4,8},{8,12},{1,5},{5,9},{9,13},{2,6},{6,10},{10,14},{3,7},{... | collective-permute-start | bytes 393224 | tf_op jit(solution)/shard_map/ppermute | solution.py:12
  21.5 7.3 %select_select_fusion = f32[16,64,512]{2,1,0:T(8,128)} fusion(s32[16,64,512]{2,1,0:T(8,128)S(1)} %copy-done.9, f32[]{:T(128)} %bitcast.12, f32[]{:T(128)} %bitcast.11, f32[]{:T(128)} %bitcast.10, f32[]{:T(128)} %bitcast.9, f32[]{:T(128)} %bitcast.8, f32[]{:T(128)} %bitcast.7, f32[]{:T(128)} %bitcast.6, f32[]{:T(128)} %bitcast.5), kind=kLoop, calls=%fused_computation.103 | loop fusion | flops 8388608 | bytes 4194336 | tf_op jit(solution)/shard_map/jit(_where)/select_n | solution.py:23
  31.0 3.2 %convolution_add_fusion.1 = f32[8,64,512]{2,1,0:T(8,128)S(1)} fusion(f32[8,64,512]{2,1,0:T(8,128)} %param.11, f32[8,64,258]{2,1,0:T(8,128)S(1)} %dot_general.10, s32[512]{0:T(512)S(1)} %get-tuple-element.53, s32[512]{0:T(512)S(1)} %get-tuple-element.54), kind=kOutput, calls=%fused_computation.117 | convolution fusion | flops 812520448 | bytes 2629632 | tf_op jit(solution)/shard_map/dot_general | solution.py:92
  34.2 4.6 %collective-permute-start.4 = (f32[1,64,512]{2,1,0:T(8,128)S(1)}, f32[1,64,512]{2,1,0:T(8,128)S(1)}, u32[]{:S(2)}, u32[]{:S(2)}) collective-permute-start(f32[1,64,512]{2,1,0:T(8,128)S(1)} %get-tuple-element.33), channel_id=1, source_target_pairs={{0,4},{4,8},{8,12},{1,5},{5,9},{9,13},{2,6},{6,10},{10,14},{3,7},{... | collective-permute-start | bytes 393224 | tf_op jit(solution)/shard_map/ppermute | solution.py:12
  41.3 4.4 %collective-permute-done.5 = f32[1,64,512]{2,1,0:T(8,128)S(1)} collective-permute-done((f32[1,64,512]{2,1,0:T(8,128)S(1)}, f32[1,64,512]{2,1,0:T(8,128)S(1)}, u32[]{:S(2)}, u32[]{:S(2)}) %collective-permute-start.5) | collective-permute-done | bytes 131104 | tf_op jit(solution)/shard_map/ppermute | solution.py:15
  46.2 3.4 %multiply_add_fusion.1 = (f32[8,64,512]{2,1,0:T(8,128)S(1)}, f32[8,64,512]{2,1,0:T(8,128)}) fusion(f32[8,64,512]{2,1,0:T(8,128)S(1)} %convolution_add_fusion.1, f32[8,64,512]{2,1,0:T(8,128)S(1)} %copy-done.5, f32[10,66,514]{2,1,0:T(8,128)S(1)} %select_maximum_fusion.2, f32[1,64,512]{2,1,0:T(8,128)S(1)} %collective-permute-done.5, ...), kind=kLoop, calls=%fused_computation.167 | loop fusion | flops 9961472 | bytes 14155776 | tf_op jit(solution)/shard_map/add | solution.py:56
  51.3 3.5 %collective-permute-start.6 = (f32[1,64,512]{2,1,0:T(8,128)}, f32[1,64,512]{2,1,0:T(8,128)S(1)}, u32[]{:S(2)}, u32[]{:S(2)}) collective-permute-start(f32[1,64,512]{2,1,0:T(8,128)} %get-tuple-element.29), channel_id=1, source_target_pairs={{0,4},{4,8},{8,12},{1,5},{5,9},{9,13},{2,6},{6,10},{10,14},{3,7},{... | collective-permute-start | bytes 393224 | tf_op jit(solution)/shard_map/ppermute | solution.py:12
  57.8 4.5 %collective-permute-start.10 = (f32[1,64,512]{2,1,0:T(8,128)}, f32[1,64,512]{2,1,0:T(8,128)S(1)}, u32[]{:S(2)}, u32[]{:S(2)}) collective-permute-start(f32[1,64,512]{2,1,0:T(8,128)} %get-tuple-element.23), channel_id=1, source_target_pairs={{0,4},{4,8},{8,12},{1,5},{5,9},{9,13},{2,6},{6,10},{10,14},{3,7},{... | collective-permute-start | bytes 393224 | tf_op jit(solution)/shard_map/ppermute | solution.py:12
  63.7 2.0 select_maximum_fusion
  65.9 3.4 %fusion.50 = f32[8,64,512]{2,1,0:T(8,128)S(1)} fusion(f32[8,64,512]{2,1,0:T(8,128)S(1)} %copy-done.4, f32[8,64,512]{2,1,0:T(8,128)S(1)} %copy-done.6, f32[10,66,514]{2,1,0:T(8,128)S(1)} %select_maximum_fusion, f32[1,64,512]{2,1,0:T(8,128)} %collective-permute-done.7, f32[1,64,512]{2,1,0:T(8,128)S(1)} %collective-permute-done.6, ...), kind=kLoop, calls=%fused_computation.124 | loop fusion | flops 10485760 | bytes 14155776 | tf_op jit(solution)/shard_map/add | solution.py:60
  70.7 5.4 %collective-permute-start.8 = (f32[1,64,512]{2,1,0:T(8,128)S(1)}, f32[1,64,512]{2,1,0:T(8,128)S(1)}, u32[]{:S(2)}, u32[]{:S(2)}) collective-permute-start(f32[1,64,512]{2,1,0:T(8,128)S(1)} %get-tuple-element.28), channel_id=1, source_target_pairs={{0,4},{4,8},{8,12},{1,5},{5,9},{9,13},{2,6},{6,10},{10,14},{3,7},{... | collective-permute-start | bytes 393224 | tf_op jit(solution)/shard_map/ppermute | solution.py:12
  82.1 2.2 %dot_general.12 = f32[16,64,258]{2,1,0:T(8,128)} reshape(f32[16,32,2,258]{3,2,1,0:T(2,128)S(1)} %copy.18) | data formatting | bytes 2113536 | tf_op jit(solution)/shard_map/dot_general | solution.py:92
  84.3 5.8 %convolution_add_fusion = f32[16,64,512]{2,1,0:T(8,128)S(1)} fusion(f32[16,64,512]{2,1,0:T(8,128)} %param.8, f32[16,64,258]{2,1,0:T(8,128)} %dot_general.12, s32[512]{0:T(512)S(1)} %get-tuple-element.53, s32[512]{0:T(512)S(1)} %get-tuple-element.54), kind=kOutput, calls=%fused_computation.115 | convolution fusion | flops 1624380416 | bytes 5255168 | tf_op jit(solution)/shard_map/dot_general | solution.py:92
  90.2 4.4 %collective-permute-start.16 = (f32[1,64,512]{2,1,0:T(8,128)S(1)}, f32[1,64,512]{2,1,0:T(8,128)S(1)}, u32[]{:S(2)}, u32[]{:S(2)}) collective-permute-start(f32[1,64,512]{2,1,0:T(8,128)S(1)} %get-tuple-element.25), channel_id=1, source_target_pairs={{0,4},{4,8},{8,12},{1,5},{5,9},{9,13},{2,6},{6,10},{10,14},{3,7},{... | collective-permute-start | bytes 393224 | tf_op jit(solution)/shard_map/ppermute | solution.py:12
  95.9 3.4 %collective-permute-start.12 = (f32[18,1,512]{2,1,0:T(1,128)S(1)}, f32[18,1,512]{2,1,0:T(1,128)S(1)}, u32[]{:S(2)}, u32[]{:S(2)}) collective-permute-start(f32[18,1,512]{2,1,0:T(1,128)S(1)} %get-tuple-element.17), channel_id=1, source_target_pairs={{0,2},{1,3},{4,6},{5,7},{8,10},{9,11},{12,14},{13,15},{16,18},{17,... | collective-permute-start | bytes 110600 | tf_op jit(solution)/shard_map/ppermute | solution.py:12
  102.1 4.4 %collective-permute-start.18 = (f32[18,1,512]{2,1,0:T(1,128)}, f32[18,1,512]{2,1,0:T(1,128)}, u32[]{:S(2)}, u32[]{:S(2)}) collective-permute-start(f32[18,1,512]{2,1,0:T(1,128)} %get-tuple-element.19), channel_id=1, source_target_pairs={{0,2},{1,3},{4,6},{5,7},{8,10},{9,11},{12,14},{13,15},{16,18},{17,... | collective-permute-start | bytes 110600 | tf_op jit(solution)/shard_map/ppermute | solution.py:12
  112.6 4.2 %collective-permute-start.14 = (f32[18,66,1]{1,2,0:T(1,128)}, f32[18,66,1]{1,2,0:T(1,128)}, u32[]{:S(2)}, u32[]{:S(2)}) collective-permute-start(f32[18,66,1]{1,2,0:T(1,128)} %copy.19), channel_id=1, source_target_pairs={{0,1},{2,3},{4,5},{6,7},{8,9},{10,11},{12,13},{14,15},{16,17},{18,... | collective-permute-start | bytes 14264 | tf_op jit(solution)/shard_map/ppermute | solution.py:12
  119.3 1.9 collective-permute-start.20
  125.6 1.9 copy.24
  129.3 20.5 %multiply_add_fusion = (f32[16,64,512]{2,1,0:T(8,128)S(1)}, f32[16,64,512]{2,1,0:T(8,128)}) fusion(f32[16,64,512]{2,1,0:T(8,128)} %copy-done.1, f32[16,64,512]{2,1,0:T(8,128)} %param.9, f32[18,66,1]{2,1,0:T(8,128)} %copy.26, f32[18,1,512]{2,1,0:T(1,128)} %collective-permute-done.19, f32[1,64,512]{2,1,0:T(8,128)} %copy-done.11, f32[1,64,512]{2,1,0:T(8,128)} %copy-done.10, ...), kind=kLoop, calls=%fused_computation.101 | loop fusion | flops 36700160 | bytes 11176512 | tf_op jit(solution)/shard_map/add | solution.py:56
  149.9 4.6 %collective-permute-start.22 = (f32[1,64,512]{2,1,0:T(8,128)S(1)}, f32[1,64,512]{2,1,0:T(8,128)S(1)}, u32[]{:S(2)}, u32[]{:S(2)}) collective-permute-start(f32[1,64,512]{2,1,0:T(8,128)S(1)} %get-tuple-element.21), channel_id=1, source_target_pairs={{0,4},{4,8},{8,12},{1,5},{5,9},{9,13},{2,6},{6,10},{10,14},{3,7},{... | collective-permute-start | bytes 393224 | tf_op jit(solution)/shard_map/ppermute | solution.py:12
  155.7 2.1 %collective-permute-done.22 = f32[1,64,512]{2,1,0:T(8,128)S(1)} collective-permute-done((f32[1,64,512]{2,1,0:T(8,128)S(1)}, f32[1,64,512]{2,1,0:T(8,128)S(1)}, u32[]{:S(2)}, u32[]{:S(2)}) %collective-permute-start.22) | collective-permute-done | bytes 131104 | tf_op jit(solution)/shard_map/ppermute | solution.py:12
  157.9 4.4 %collective-permute-done.23 = f32[1,64,512]{2,1,0:T(8,128)S(1)} collective-permute-done((f32[1,64,512]{2,1,0:T(8,128)S(1)}, f32[1,64,512]{2,1,0:T(8,128)S(1)}, u32[]{:S(2)}, u32[]{:S(2)}) %collective-permute-start.23) | collective-permute-done | bytes 131104 | tf_op jit(solution)/shard_map/ppermute | solution.py:15
  162.3 5.1 %collective-permute-start.24 = (f32[18,1,512]{2,1,0:T(1,128)S(1)}, f32[18,1,512]{2,1,0:T(1,128)S(1)}, u32[]{:S(2)}, u32[]{:S(2)}) collective-permute-start(f32[18,1,512]{2,1,0:T(1,128)S(1)} %get-tuple-element.15), channel_id=1, source_target_pairs={{0,2},{1,3},{4,6},{5,7},{8,10},{9,11},{12,14},{13,15},{16,18},{17,... | collective-permute-start | bytes 110600 | tf_op jit(solution)/shard_map/ppermute | solution.py:12
  169.1 4.2 %collective-permute-done.25 = f32[18,1,512]{2,1,0:T(1,128)S(1)} collective-permute-done((f32[18,1,512]{2,1,0:T(1,128)S(1)}, f32[18,1,512]{2,1,0:T(1,128)S(1)}, u32[]{:S(2)}, u32[]{:S(2)}) %collective-permute-start.25) | collective-permute-done | bytes 36896 | tf_op jit(solution)/shard_map/ppermute | solution.py:15
  174.8 2.0 copy.27
  176.7 1.9 collective-permute-start.26
  178.6 2.0 copy.29
  181.8 1.9 copy.28
  185.8 21.1 %fusion.6 = f32[16,64,512]{2,1,0:T(8,128)} fusion(f32[16,64,512]{2,1,0:T(8,128)} %copy-done.2, f32[16,64,512]{2,1,0:T(8,128)} %param.9, f32[18,66,1]{2,1,0:T(8,128)} %copy.30, f32[18,1,512]{2,1,0:T(1,128)} %copy-done.18, f32[18,1,512]{2,1,0:T(1,128)} %copy-done.17, f32[1,64,512]{2,1,0:T(8,128)} %copy-done.13, f32[1,64,512]{2,1,0:T(8,128)} %copy-done.12, ...), kind=kLoop, calls=%fused_computation.11 | loop fusion | flops 37748736 | bytes 11176512 | tf_op jit(solution)/shard_map/add | solution.py:60
  (120 shorter events, 50.6 us)
Async XLA Ops:
  0.0 21.5 %copy-start.9 = (s32[16,64,512]{2,1,0:T(8,128)S(1)}, s32[16,64,512]{2,1,0:T(8,128)}, u32[]{:S(2)}) copy-start(s32[16,64,512]{2,1,0:T(8,128)} %param.10) | copy-start | bytes 6291460
  0.9 27.9 %collective-permute-start = (f32[1,32,256]{2,1,0:T(8,128)S(1)}, f32[1,32,256]{2,1,0:T(8,128)S(1)}, u32[]{:S(2)}, u32[]{:S(2)}) collective-permute-start(f32[1,32,256]{2,1,0:T(8,128)S(1)} %get-tuple-element.43), channel_id=1, source_target_pairs={{0,4},{4,8},{8,12},{1,5},{5,9},{9,13},{2,6},{6,10},{10,14},{3,7},{... | collective-permute-start | bytes 98312 | tf_op jit(solution)/shard_map/ppermute | solution.py:12
  5.9 22.9 %collective-permute-start.1 = (f32[1,32,256]{2,1,0:T(8,128)S(1)}, f32[1,32,256]{2,1,0:T(8,128)S(1)}, u32[]{:S(2)}, u32[]{:S(2)}) collective-permute-start(f32[1,32,256]{2,1,0:T(8,128)S(1)} %get-tuple-element.44), channel_id=1, source_target_pairs={{4,0},{8,4},{12,8},{5,1},{9,5},{13,9},{6,2},{10,6},{14,10},{7,3},{... | collective-permute-start | bytes 98312 | tf_op jit(solution)/shard_map/ppermute | solution.py:15
  15.5 24.6 %collective-permute-start.2 = (f32[1,64,512]{2,1,0:T(8,128)S(1)}, f32[1,64,512]{2,1,0:T(8,128)S(1)}, u32[]{:S(2)}, u32[]{:S(2)}) collective-permute-start(f32[1,64,512]{2,1,0:T(8,128)S(1)} %get-tuple-element.31), channel_id=1, source_target_pairs={{0,4},{4,8},{8,12},{1,5},{5,9},{9,13},{2,6},{6,10},{10,14},{3,7},{... | collective-permute-start | bytes 393224 | tf_op jit(solution)/shard_map/ppermute | solution.py:12
  20.0 20.0 %collective-permute-start.3 = (f32[1,64,512]{2,1,0:T(8,128)S(1)}, f32[1,64,512]{2,1,0:T(8,128)S(1)}, u32[]{:S(2)}, u32[]{:S(2)}) collective-permute-start(f32[1,64,512]{2,1,0:T(8,128)S(1)} %get-tuple-element.32), channel_id=1, source_target_pairs={{4,0},{8,4},{12,8},{5,1},{9,5},{13,9},{6,2},{10,6},{14,10},{7,3},{... | collective-permute-start | bytes 393224 | tf_op jit(solution)/shard_map/ppermute | solution.py:15
  34.2 7.1 %collective-permute-start.4 = (f32[1,64,512]{2,1,0:T(8,128)S(1)}, f32[1,64,512]{2,1,0:T(8,128)S(1)}, u32[]{:S(2)}, u32[]{:S(2)}) collective-permute-start(f32[1,64,512]{2,1,0:T(8,128)S(1)} %get-tuple-element.33), channel_id=1, source_target_pairs={{0,4},{4,8},{8,12},{1,5},{5,9},{9,13},{2,6},{6,10},{10,14},{3,7},{... | collective-permute-start | bytes 393224 | tf_op jit(solution)/shard_map/ppermute | solution.py:12
  38.8 6.9 %collective-permute-start.5 = (f32[1,64,512]{2,1,0:T(8,128)S(1)}, f32[1,64,512]{2,1,0:T(8,128)S(1)}, u32[]{:S(2)}, u32[]{:S(2)}) collective-permute-start(f32[1,64,512]{2,1,0:T(8,128)S(1)} %get-tuple-element.34), channel_id=1, source_target_pairs={{4,0},{8,4},{12,8},{5,1},{9,5},{13,9},{6,2},{10,6},{14,10},{7,3},{... | collective-permute-start | bytes 393224 | tf_op jit(solution)/shard_map/ppermute | solution.py:15
  51.3 12.4 %collective-permute-start.6 = (f32[1,64,512]{2,1,0:T(8,128)}, f32[1,64,512]{2,1,0:T(8,128)S(1)}, u32[]{:S(2)}, u32[]{:S(2)}) collective-permute-start(f32[1,64,512]{2,1,0:T(8,128)} %get-tuple-element.29), channel_id=1, source_target_pairs={{0,4},{4,8},{8,12},{1,5},{5,9},{9,13},{2,6},{6,10},{10,14},{3,7},{... | collective-permute-start | bytes 393224 | tf_op jit(solution)/shard_map/ppermute | solution.py:12
  54.8 8.9 %collective-permute-start.7 = (f32[1,64,512]{2,1,0:T(8,128)}, f32[1,64,512]{2,1,0:T(8,128)}, u32[]{:S(2)}, u32[]{:S(2)}) collective-permute-start(f32[1,64,512]{2,1,0:T(8,128)} %get-tuple-element.30), channel_id=1, source_target_pairs={{4,0},{8,4},{12,8},{5,1},{9,5},{13,9},{6,2},{10,6},{14,10},{7,3},{... | collective-permute-start | bytes 393224 | tf_op jit(solution)/shard_map/ppermute | solution.py:15
  57.8 38.0 %collective-permute-start.10 = (f32[1,64,512]{2,1,0:T(8,128)}, f32[1,64,512]{2,1,0:T(8,128)S(1)}, u32[]{:S(2)}, u32[]{:S(2)}) collective-permute-start(f32[1,64,512]{2,1,0:T(8,128)} %get-tuple-element.23), channel_id=1, source_target_pairs={{0,4},{4,8},{8,12},{1,5},{5,9},{9,13},{2,6},{6,10},{10,14},{3,7},{... | collective-permute-start | bytes 393224 | tf_op jit(solution)/shard_map/ppermute | solution.py:12
  62.3 33.5 %collective-permute-start.11 = (f32[1,64,512]{2,1,0:T(8,128)}, f32[1,64,512]{2,1,0:T(8,128)S(1)}, u32[]{:S(2)}, u32[]{:S(2)}) collective-permute-start(f32[1,64,512]{2,1,0:T(8,128)} %get-tuple-element.24), channel_id=1, source_target_pairs={{4,0},{8,4},{12,8},{5,1},{9,5},{13,9},{6,2},{10,6},{14,10},{7,3},{... | collective-permute-start | bytes 393224 | tf_op jit(solution)/shard_map/ppermute | solution.py:15
  69.4 7.5 %collective-permute-start.9 = (f32[1,64,512]{2,1,0:T(8,128)S(1)}, f32[1,64,512]{2,1,0:T(8,128)S(1)}, u32[]{:S(2)}, u32[]{:S(2)}) collective-permute-start(f32[1,64,512]{2,1,0:T(8,128)S(1)} %get-tuple-element.27), channel_id=1, source_target_pairs={{4,0},{8,4},{12,8},{5,1},{9,5},{13,9},{6,2},{10,6},{14,10},{7,3},{... | collective-permute-start | bytes 393224 | tf_op jit(solution)/shard_map/ppermute | solution.py:15
  70.7 7.7 %collective-permute-start.8 = (f32[1,64,512]{2,1,0:T(8,128)S(1)}, f32[1,64,512]{2,1,0:T(8,128)S(1)}, u32[]{:S(2)}, u32[]{:S(2)}) collective-permute-start(f32[1,64,512]{2,1,0:T(8,128)S(1)} %get-tuple-element.28), channel_id=1, source_target_pairs={{0,4},{4,8},{8,12},{1,5},{5,9},{9,13},{2,6},{6,10},{10,14},{3,7},{... | collective-permute-start | bytes 393224 | tf_op jit(solution)/shard_map/ppermute | solution.py:12
  90.2 10.5 %collective-permute-start.16 = (f32[1,64,512]{2,1,0:T(8,128)S(1)}, f32[1,64,512]{2,1,0:T(8,128)S(1)}, u32[]{:S(2)}, u32[]{:S(2)}) collective-permute-start(f32[1,64,512]{2,1,0:T(8,128)S(1)} %get-tuple-element.25), channel_id=1, source_target_pairs={{0,4},{4,8},{8,12},{1,5},{5,9},{9,13},{2,6},{6,10},{10,14},{3,7},{... | collective-permute-start | bytes 393224 | tf_op jit(solution)/shard_map/ppermute | solution.py:12
  94.5 6.9 %collective-permute-start.17 = (f32[1,64,512]{2,1,0:T(8,128)S(1)}, f32[1,64,512]{2,1,0:T(8,128)S(1)}, u32[]{:S(2)}, u32[]{:S(2)}) collective-permute-start(f32[1,64,512]{2,1,0:T(8,128)S(1)} %get-tuple-element.26), channel_id=1, source_target_pairs={{4,0},{8,4},{12,8},{5,1},{9,5},{13,9},{6,2},{10,6},{14,10},{7,3},{... | collective-permute-start | bytes 393224 | tf_op jit(solution)/shard_map/ppermute | solution.py:15
  95.9 11.9 %collective-permute-start.12 = (f32[18,1,512]{2,1,0:T(1,128)S(1)}, f32[18,1,512]{2,1,0:T(1,128)S(1)}, u32[]{:S(2)}, u32[]{:S(2)}) collective-permute-start(f32[18,1,512]{2,1,0:T(1,128)S(1)} %get-tuple-element.17), channel_id=1, source_target_pairs={{0,2},{1,3},{4,6},{5,7},{8,10},{9,11},{12,14},{13,15},{16,18},{17,... | collective-permute-start | bytes 110600 | tf_op jit(solution)/shard_map/ppermute | solution.py:12
  99.3 8.5 %collective-permute-start.13 = (f32[18,1,512]{2,1,0:T(1,128)S(1)}, f32[18,1,512]{2,1,0:T(1,128)S(1)}, u32[]{:S(2)}, u32[]{:S(2)}) collective-permute-start(f32[18,1,512]{2,1,0:T(1,128)S(1)} %get-tuple-element.18), channel_id=1, source_target_pairs={{2,0},{3,1},{6,4},{7,5},{10,8},{11,9},{14,12},{15,13},{18,16},{19,... | collective-permute-start | bytes 110600 | tf_op jit(solution)/shard_map/ppermute | solution.py:15
  102.1 14.7 %collective-permute-start.18 = (f32[18,1,512]{2,1,0:T(1,128)}, f32[18,1,512]{2,1,0:T(1,128)}, u32[]{:S(2)}, u32[]{:S(2)}) collective-permute-start(f32[18,1,512]{2,1,0:T(1,128)} %get-tuple-element.19), channel_id=1, source_target_pairs={{0,2},{1,3},{4,6},{5,7},{8,10},{9,11},{12,14},{13,15},{16,18},{17,... | collective-permute-start | bytes 110600 | tf_op jit(solution)/shard_map/ppermute | solution.py:12
  106.5 10.3 %collective-permute-start.19 = (f32[18,1,512]{2,1,0:T(1,128)}, f32[18,1,512]{2,1,0:T(1,128)}, u32[]{:S(2)}, u32[]{:S(2)}) collective-permute-start(f32[18,1,512]{2,1,0:T(1,128)} %get-tuple-element.20), channel_id=1, source_target_pairs={{2,0},{3,1},{6,4},{7,5},{10,8},{11,9},{14,12},{15,13},{18,16},{19,... | collective-permute-start | bytes 110600 | tf_op jit(solution)/shard_map/ppermute | solution.py:15
  111.3 13.3 %collective-permute-start.15 = (f32[18,66,1]{1,2,0:T(1,128)}, f32[18,66,1]{1,2,0:T(1,128)}, u32[]{:S(2)}, u32[]{:S(2)}) collective-permute-start(f32[18,66,1]{1,2,0:T(1,128)} %copy.21), channel_id=1, source_target_pairs={{1,0},{3,2},{5,4},{7,6},{9,8},{11,10},{13,12},{15,14},{17,16},{19,... | collective-permute-start | bytes 14264 | tf_op jit(solution)/shard_map/ppermute | solution.py:15
  112.6 10.9 %collective-permute-start.14 = (f32[18,66,1]{1,2,0:T(1,128)}, f32[18,66,1]{1,2,0:T(1,128)}, u32[]{:S(2)}, u32[]{:S(2)}) collective-permute-start(f32[18,66,1]{1,2,0:T(1,128)} %copy.19), channel_id=1, source_target_pairs={{0,1},{2,3},{4,5},{6,7},{8,9},{10,11},{12,13},{14,15},{16,17},{18,... | collective-permute-start | bytes 14264 | tf_op jit(solution)/shard_map/ppermute | solution.py:12
  119.3 6.3 %collective-permute-start.20 = (f32[18,66,1]{1,2,0:T(1,128)}, f32[18,66,1]{1,2,0:T(1,128)}, u32[]{:S(2)}, u32[]{:S(2)}) collective-permute-start(f32[18,66,1]{1,2,0:T(1,128)} %copy.23), channel_id=1, source_target_pairs={{0,1},{2,3},{4,5},{6,7},{8,9},{10,11},{12,13},{14,15},{16,17},{18,... | collective-permute-start | bytes 14264 | tf_op jit(solution)/shard_map/ppermute | solution.py:12
  122.0 5.5 %collective-permute-start.21 = (f32[18,66,1]{1,2,0:T(1,128)}, f32[18,66,1]{1,2,0:T(1,128)}, u32[]{:S(2)}, u32[]{:S(2)}) collective-permute-start(f32[18,66,1]{1,2,0:T(1,128)} %copy.25), channel_id=1, source_target_pairs={{1,0},{3,2},{5,4},{7,6},{9,8},{11,10},{13,12},{15,14},{17,16},{19,... | collective-permute-start | bytes 14264 | tf_op jit(solution)/shard_map/ppermute | solution.py:15
  149.8 24.9 %copy-start.2 = (f32[16,64,512]{2,1,0:T(8,128)}, f32[16,64,512]{2,1,0:T(8,128)S(1)}, u32[]{:S(2)}) copy-start(f32[16,64,512]{2,1,0:T(8,128)S(1)} %get-tuple-element.5) | copy-start | bytes 6291460
  149.9 8.0 %collective-permute-start.22 = (f32[1,64,512]{2,1,0:T(8,128)S(1)}, f32[1,64,512]{2,1,0:T(8,128)S(1)}, u32[]{:S(2)}, u32[]{:S(2)}) collective-permute-start(f32[1,64,512]{2,1,0:T(8,128)S(1)} %get-tuple-element.21), channel_id=1, source_target_pairs={{0,4},{4,8},{8,12},{1,5},{5,9},{9,13},{2,6},{6,10},{10,14},{3,7},{... | collective-permute-start | bytes 393224 | tf_op jit(solution)/shard_map/ppermute | solution.py:12
  154.4 7.8 %collective-permute-start.23 = (f32[1,64,512]{2,1,0:T(8,128)S(1)}, f32[1,64,512]{2,1,0:T(8,128)S(1)}, u32[]{:S(2)}, u32[]{:S(2)}) collective-permute-start(f32[1,64,512]{2,1,0:T(8,128)S(1)} %get-tuple-element.22), channel_id=1, source_target_pairs={{4,0},{8,4},{12,8},{5,1},{9,5},{13,9},{6,2},{10,6},{14,10},{7,3},{... | collective-permute-start | bytes 393224 | tf_op jit(solution)/shard_map/ppermute | solution.py:15
  157.9 16.9 %copy-start.12 = (f32[1,64,512]{2,1,0:T(8,128)}, f32[1,64,512]{2,1,0:T(8,128)S(1)}, u32[]{:S(2)}) copy-start(f32[1,64,512]{2,1,0:T(8,128)S(1)} %collective-permute-done.22) | copy-start | bytes 393220
  162.3 12.5 %copy-start.13 = (f32[1,64,512]{2,1,0:T(8,128)}, f32[1,64,512]{2,1,0:T(8,128)S(1)}, u32[]{:S(2)}) copy-start(f32[1,64,512]{2,1,0:T(8,128)S(1)} %collective-permute-done.23) | copy-start | bytes 393220
  162.3 6.7 %collective-permute-start.24 = (f32[18,1,512]{2,1,0:T(1,128)S(1)}, f32[18,1,512]{2,1,0:T(1,128)S(1)}, u32[]{:S(2)}, u32[]{:S(2)}) collective-permute-start(f32[18,1,512]{2,1,0:T(1,128)S(1)} %get-tuple-element.15), channel_id=1, source_target_pairs={{0,2},{1,3},{4,6},{5,7},{8,10},{9,11},{12,14},{13,15},{16,18},{17,... | collective-permute-start | bytes 110600 | tf_op jit(solution)/shard_map/ppermute | solution.py:12
  167.5 5.9 %collective-permute-start.25 = (f32[18,1,512]{2,1,0:T(1,128)S(1)}, f32[18,1,512]{2,1,0:T(1,128)S(1)}, u32[]{:S(2)}, u32[]{:S(2)}) collective-permute-start(f32[18,1,512]{2,1,0:T(1,128)S(1)} %get-tuple-element.16), channel_id=1, source_target_pairs={{2,0},{3,1},{6,4},{7,5},{10,8},{11,9},{14,12},{15,13},{18,16},{19,... | collective-permute-start | bytes 110600 | tf_op jit(solution)/shard_map/ppermute | solution.py:15
  176.7 5.1 %collective-permute-start.26 = (f32[18,66,1]{1,2,0:T(1,128)}, f32[18,66,1]{1,2,0:T(1,128)}, u32[]{:S(2)}, u32[]{:S(2)}) collective-permute-start(f32[18,66,1]{1,2,0:T(1,128)} %copy.27), channel_id=1, source_target_pairs={{0,1},{2,3},{4,5},{6,7},{8,9},{10,11},{12,13},{14,15},{16,17},{18,... | collective-permute-start | bytes 14264 | tf_op jit(solution)/shard_map/ppermute | solution.py:12
  180.5 3.4 %collective-permute-start.27 = (f32[18,66,1]{1,2,0:T(1,128)}, f32[18,66,1]{1,2,0:T(1,128)}, u32[]{:S(2)}, u32[]{:S(2)}) collective-permute-start(f32[18,66,1]{1,2,0:T(1,128)} %copy.29), channel_id=1, source_target_pairs={{1,0},{3,2},{5,4},{7,6},{9,8},{11,10},{13,12},{15,14},{17,16},{19,... | collective-permute-start | bytes 14264 | tf_op jit(solution)/shard_map/ppermute | solution.py:15
  (15 other events, 72.5 us)
where the time goes:
time: 210 us; the launch traced here: 207 us
  starting transfers between devices  75.6 us (36%)
  other arithmetic  72.3 us (34%)
  local copies, waits for them, and re-layouts  30.2 us (14%)
  waiting for transfers between devices  19.1 us (9%)
  matrix products  8.99 us (4%)
    ppermute x14, starting transfers between devices, extended(): lax.ppermute(lax.slice_in_dim(block, block.shape[dim] - width, None, axis...  57.2 us
    add x2, other arithmetic, smooth(): return field + step_two  24.5 us
    add x2, other arithmetic, smooth(): field = first_ext[1:-1, 1:-1, 1:-1] + step_one  23.9 us
    ppermute x14, starting transfers between devices, extended(): lax.ppermute(lax.slice_in_dim(block, 0, width, axis=dim), axis, backward)  18.4 us
    ppermute x14, waiting for transfers between devices, extended(): lax.ppermute(lax.slice_in_dim(block, 0, width, axis=dim), axis, backward)  14.5 us
    select_n x2, other arithmetic, lookup(): kappa = jnp.where(ids == material, table[material], kappa)  14 us
    dot_general x2, matrix products, prolong(): jnp.dot(flat, matrix, precision=lax.Precision.HIGHEST, preferred_element_...  8.99 us
    slice x10, local copies, waits for them, and re-layouts, extended(): lax.slice_in_dim(block, block.shape[dim] - width, None, axis=dim)  7.11 us
  transfers between devices with their start and end apart: 28, of which 10 were waited for; matrix products, arithmetic and copies ran while one was open for 27% of the time, Pallas kernels for 0%

commit v1 on v0

v1 whole, which is shorter than its diff:
```python
import functools

import jax
import jax.numpy as jnp
from jax import lax
from jax.experimental import pallas as pl
from jax.experimental.pallas import tpu as pltpu
from jax.sharding import PartitionSpec as P

F32 = jnp.float32
HI = lax.Precision.HIGHEST


def lookup(ids, table):
    kappa = jnp.zeros(ids.shape, F32)
    for material, value in enumerate(table):
        kappa = jnp.where(ids == material, value, kappa)
    return kappa


def weights_of(shape, fine_axis, first, total, offset, wrap=None):
    fine = lax.broadcasted_iota(jnp.int32, shape, fine_axis)
    if wrap is not None:
        fine = jnp.where(fine >= wrap[0], fine - wrap[1], fine)
    fine = fine + first
    base = fine >> 1
    side = base + 2 * (fine & 1) - 1
    coarse = lax.broadcasted_iota(jnp.int32, shape, 1 - fine_axis) + offset
    main = jnp.where(coarse == base, 0.75, 0.0)
    both = jnp.where(coarse == side, 0.25, main)
    return jnp.where((fine >= 0) & (fine < total), both, 0.0).astype(F32)


def inverse(kappa, around):
    return jnp.where(kappa > 0.0, 1.0 / (6.0 * kappa + around), 0.0)


def kernel(
    sizes,
    fi_hbm, fr_hbm, fid_hbm, li_hbm, lr_hbm, lid_hbm, co_hbm, table_ref,
    out_ref,
    fi, fr, fid, fiz, fidz, fix, fidx, ysend, yidsend, yrecv, yidrecv,
    li, lr, lid, co, xc,
    lk, lv, lkv, lv1, lkv1, linv, mid, pm,
    fk, fv, fkv, fv1, fkv1, finv, vx, vysend, vyrecv,
    local_sem, send_sem, recv_sem,
):
    count_z, count_y, wr, wc = sizes
    depth, rows, cols = fi.shape
    ldepth, lrows, lcols = li_hbm.shape
    crows, ccols = co_hbm.shape[1:]
    gx = lax.axis_index("gx")
    gy = lax.axis_index("gy")
    wa = lax.axis_index("wa")
    has_zm, has_zp = gx > 0, gx < count_z - 1
    has_ym, has_yp = gy > 0, gy < count_y - 1
    row0 = pl.multiple_of(jnp.clip(gy * (rows // 2) - 8, 0, lrows - wr), 8)
    col0 = pl.multiple_of(wa * (lcols - wc), 128)
    zm, zp = {"gx": gx - 1}, {"gx": gx + 1}
    ym, yp = {"gy": gy - 1}, {"gy": gy + 1}
    other = {"wa": 1 - wa}

    barrier = pltpu.get_barrier_semaphore()
    sides = ((has_zm, zm), (has_zp, zp), (has_ym, ym), (has_yp, yp))
    for there, who in sides:
        @pl.when(there)
        def _(who=who):
            pl.semaphore_signal(barrier, 1, device_id=who, device_id_type=pl.DeviceIdType.MESH)
    pl.semaphore_signal(barrier, 1, device_id=other, device_id_type=pl.DeviceIdType.MESH)

    local = []
    for src, dst in (
        (co_hbm, co.at[pl.ds(2, ldepth // 2)]),
        (li_hbm.at[:, pl.ds(row0, wr), pl.ds(col0, wc)], li.at[pl.ds(3, ldepth)]),
        (lid_hbm.at[:, pl.ds(row0, wr), pl.ds(col0, wc)], lid.at[pl.ds(3, ldepth)]),
        (lr_hbm.at[:, pl.ds(row0, wr), pl.ds(col0, wc)], lr.at[pl.ds(2, ldepth)]),
        (fi_hbm, fi), (fid_hbm, fid), (fr_hbm, fr),
    ):
        copy = pltpu.make_async_copy(src, dst, local_sem.at[len(local)])
        copy.start()
        local.append(copy)

    present = [jnp.where(there, 1, 0) for there, _ in sides]
    pl.semaphore_wait(barrier, present[0] + present[1] + present[2] + present[3] + 1)

    used = [0]

    def send(src, dst, who, to_there, from_there):
        index = used[0]
        used[0] += 1
        copy = pltpu.make_async_remote_copy(
            src_ref=src, dst_ref=dst, send_sem=send_sem.at[index], recv_sem=recv_sem.at[index],
            device_id=who, device_id_type=pl.DeviceIdType.MESH,
        )
        if to_there is None:
            copy.start()
        else:
            pl.when(to_there)(copy.start)
        return copy, to_there, from_there

    def receive(copies):
        for copy, _, there in copies:
            if there is None:
                copy.wait_recv()
            else:
                pl.when(there)(copy.wait_recv)

    def sent(copies):
        for copy, there, _ in copies:
            if there is None:
                copy.wait_send()
            else:
                pl.when(there)(copy.wait_send)

    def z_pair(src, dst, width, own):
        count = src.shape[0]
        win = (pl.ds(row0, wr), pl.ds(col0, wc)) if dst.shape[1] == wr else (slice(None), slice(None))
        return [
            send(src.at[(pl.ds(count - width, width),) + win], dst.at[pl.ds(own - width, width)], zp, has_zp, has_zm),
            send(src.at[(pl.ds(0, width),) + win], dst.at[pl.ds(own + count, width)], zm, has_zm, has_zp),
        ]

    level_in = z_pair(co_hbm, co, 2, 2)
    level_in += z_pair(li_hbm, li, 3, 3)
    level_in += z_pair(lid_hbm, lid, 3, 3)
    level_in += z_pair(lr_hbm, lr, 2, 2)
    edge0 = pl.multiple_of((1 - wa) * (cols - 128), 128)
    fine_in = [
        send(fid_hbm.at[:, :, pl.ds(edge0, 128)], fidx, other, None, None),
        send(fi_hbm.at[:, :, pl.ds(edge0, 128)], fix, other, None, None),
    ]
    for src, dst in ((fid_hbm, fidz), (fi_hbm, fiz)):
        fine_in.append(send(src.at[pl.ds(depth - 1, 1)], dst.at[pl.ds(0, 1)], zp, has_zp, has_zm))
        fine_in.append(send(src.at[pl.ds(0, 1)], dst.at[pl.ds(1, 1)], zm, has_zm, has_zp))
    local[4].wait()
    local[5].wait()
    for src, pack, dst in ((fid, yidsend, yidrecv), (fi, ysend, yrecv)):
        for z in range(depth):
            pack[0, pl.ds(z, 1), :] = src[z, pl.ds(rows - 1, 1), :]
            pack[1, pl.ds(z, 1), :] = src[z, pl.ds(0, 1), :]
        fine_in.append(send(pack.at[0], dst.at[0], yp, has_yp, has_ym))
        fine_in.append(send(pack.at[1], dst.at[1], ym, has_ym, has_yp))

    table = [table_ref[m] for m in range(table_ref.shape[0])]
    mx = weights_of((ccols, wc), 1, col0, lcols, 0)
    my = weights_of((wr, crows), 0, row0, lrows, 0)
    mx2 = weights_of((wc, cols + 128), 1, wa * cols, 2 * lcols, col0, (cols + 64, cols + 128))
    my2 = weights_of((rows + 16, wr), 0, gy * rows - 8, 2 * lrows, row0)

    for copy in local[:4]:
        copy.wait()
    receive(level_in)

    planes = ldepth + 6
    for p in range(ldepth // 2 + 4):
        field = co[p]
        if p < 2:
            field = jnp.where(has_zm, field, 0.0)
        if p >= ldepth // 2 + 2:
            field = jnp.where(has_zp, field, 0.0)
        xc[p] = jnp.dot(field, mx, precision=HI, preferred_element_type=F32)
    lrow = lax.broadcasted_iota(jnp.int32, (wr, wc), 0)
    lcol = lax.broadcasted_iota(jnp.int32, (wr, wc), 1)
    inside = (lrow != jnp.where(gy == 0, wr - 1, 0)) & (lcol != jnp.where(wa == 0, wc - 1, 0))

    def level_start(p, carry):
        base = (p + 1) // 2
        side = base + 2 * ((p + 1) % 2) - 1
        spread = jnp.dot(my, 0.75 * xc[base] + 0.25 * xc[side], precision=HI, preferred_element_type=F32)
        here = ((p >= 3) | has_zm) & ((p < ldepth + 3) | has_zp)
        keep = inside & here
        kappa = jnp.where(keep, lookup(lid[p], table), 0.0)
        field = jnp.where(keep, li[p] + spread, 0.0)
        lk[p] = kappa
        lv[p] = field
        lkv[p] = kappa * field
        return carry

    lax.fori_loop(0, planes, level_start, 0)

    def level_sum(ref, p):
        field = ref[p]
        return (
            pltpu.roll(field, 1, 0) + pltpu.roll(field, wr - 1, 0)
            + pltpu.roll(field, 1, 1) + pltpu.roll(field, wc - 1, 1)
            + ref[p - 1] + ref[p + 1]
        )

    def level_one(p, carry):
        kappa = lk[p]
        inv = inverse(kappa, level_sum(lk, p))
        linv[p] = inv
        rhs = jnp.where(inv > 0.0, lr[p - 1], 0.0)
        goal = (2.0 * rhs + kappa * level_sum(lv, p) + level_sum(lkv, p)) * inv
        field = lv[p]
        new = field + (goal - field) * (1.0 / 1.2)
        lv1[p] = new
        lkv1[p] = kappa * new
        return carry

    lax.fori_loop(1, planes - 1, level_one, 0)

    def level_two(p, carry):
        inv = linv[p]
        rhs = jnp.where(inv > 0.0, lr[p - 1], 0.0)
        goal = (2.0 * rhs + lk[p] * level_sum(lv1, p) + level_sum(lkv1, p)) * inv
        settled = (3.0 / 14.0) * lv1[p] - (2.0 / 7.0) * lv[p] + (15.0 / 14.0) * goal
        mid[...] = jnp.dot(settled, mx2, precision=HI, preferred_element_type=F32)
        pm[p - 2] = jnp.dot(my2, mid[...], precision=HI, preferred_element_type=F32)
        return carry

    lax.fori_loop(2, planes - 2, level_two, 0)

    local[6].wait()
    receive(fine_in)
    lanes = lax.broadcasted_iota(jnp.int32, (16, 128), 1)
    edge_in = jnp.where(wa == 0, 0, 64)
    edge_in = (lanes >= edge_in) & (lanes < edge_in + 64)

    def spread_at(j, where, width):
        base = (j + 1) // 2
        side = base + 2 * ((j + 1) % 2) - 1
        return 0.75 * pm[(base,) + where + (width,)] + 0.25 * pm[(side,) + where + (width,)]

    main = slice(0, cols)
    rim = slice(cols, cols + 128)

    def put(j, where, width, kappa, field):
        fk[(j,) + where + (width,)] = kappa
        fv[(j,) + where + (width,)] = field
        fkv[(j,) + where + (width,)] = kappa * field

    for n, j, there in ((0, 0, has_zm), (1, depth + 1, has_zp)):
        for r in range(0, rows, 16):
            at = (pl.ds(8 + r, 16),)
            put(
                j, at, main,
                jnp.where(there, lookup(fidz[n, r:r + 16, :], table), 0.0),
                jnp.where(there, fiz[n, r:r + 16, :] + spread_at(j, at, main), 0.0),
            )

    def fine_start(j, carry):
        for r in range(0, rows, 16):
            at = (pl.ds(8 + r, 16),)
            put(
                j, at, main,
                lookup(fid[j - 1, r:r + 16, :], table),
                fi[j - 1, r:r + 16, :] + spread_at(j, at, main),
            )
            put(
                j, at, rim,
                jnp.where(edge_in, lookup(fidx[j - 1, r:r + 16, :], table), 0.0),
                jnp.where(edge_in, fix[j - 1, r:r + 16, :] + spread_at(j, at, rim), 0.0),
            )
        for n, row, there in ((0, 7, has_ym), (1, rows + 8, has_yp)):
            at = (pl.ds(row, 1),)
            put(
                j, at, main,
                jnp.where(there, lookup(yidrecv[n, pl.ds(j - 1, 1), :], table), 0.0),
                jnp.where(there, yrecv[n, pl.ds(j - 1, 1), :] + spread_at(j, at, main), 0.0),
            )
        return carry

    lax.fori_loop(1, depth + 1, fine_start, 0)

    def fine_sum(ref, j, r):
        centre = ref[j, r:r + 16, :]
        return (
            pltpu.roll(centre, 1, 1)[:, :cols] + pltpu.roll(centre, cols + 127, 1)[:, :cols]
            + ref[j, r - 1:r + 15, main] + ref[j, r + 1:r + 17, main]
            + ref[j - 1, r:r + 16, main] + ref[j + 1, r:r + 16, main]
        )

    def fine_one(j, carry):
        for r in range(0, rows, 16):
            s = 8 + r
            kappa = fk[j, s:s + 16, main]
            inv = 1.0 / (6.0 * kappa + fine_sum(fk, j, s))
            finv[j - 1, r:r + 16, :] = inv
            goal = (2.0 * fr[j - 1, r:r + 16, :] + kappa * fine_sum(fv, j, s) + fine_sum(fkv, j, s)) * inv
            field = fv[j, s:s + 16, main]
            new = field + (goal - field) * (1.0 / 1.2)
            fv1[j, s:s + 16, main] = new
            fkv1[j, s:s + 16, main] = kappa * new
        return carry

    lax.fori_loop(1, depth + 1, fine_one, 0)

    own = pl.ds(8, rows)
    fine_out = [
        send(fv1.at[pl.ds(depth, 1), own, pl.ds(0, cols)], fv1.at[pl.ds(0, 1), own, pl.ds(0, cols)], zp, has_zp, has_zm),
        send(fv1.at[pl.ds(1, 1), own, pl.ds(0, cols)], fv1.at[pl.ds(depth + 1, 1), own, pl.ds(0, cols)], zm, has_zm, has_zp),
        send(fv1.at[pl.ds(1, depth), own, pl.ds(edge0, 128)], vx, other, None, None),
    ]
    for z in range(depth):
        vysend[0, pl.ds(z, 1), :] = fv1[z + 1, pl.ds(rows + 7, 1), main]
        vysend[1, pl.ds(z, 1), :] = fv1[z + 1, pl.ds(8, 1), main]
    fine_out.append(send(vysend.at[0], vyrecv.at[0], yp, has_yp, has_ym))
    fine_out.append(send(vysend.at[1], vyrecv.at[1], ym, has_ym, has_yp))
    receive(fine_out)

    for j, there in ((0, has_zm), (depth + 1, has_zp)):
        for r in range(8, rows + 8, 16):
            field = jnp.where(there, fv1[j, r:r + 16, main], 0.0)
            fv1[j, r:r + 16, main] = field
            fkv1[j, r:r + 16, main] = fk[j, r:r + 16, main] * field

    def fine_rims(j, carry):
        for r in range(0, rows, 16):
            s = 8 + r
            field = jnp.where(edge_in, vx[j - 1, r:r + 16, :], 0.0)
            fv1[j, s:s + 16, rim] = field
            fkv1[j, s:s + 16, rim] = fk[j, s:s + 16, rim] * field
        for n, row, there in ((0, 7, has_ym), (1, rows + 8, has_yp)):
            field = jnp.where(there, vyrecv[n, pl.ds(j - 1, 1), :], 0.0)
            fv1[j, pl.ds(row, 1), main] = field
            fkv1[j, pl.ds(row, 1), main] = fk[j, pl.ds(row, 1), main] * field
        return carry

    lax.fori_loop(1, depth + 1, fine_rims, 0)

    def fine_two(j, carry):
        for r in range(0, rows, 16):
            s = 8 + r
            goal = (
                2.0 * fr[j - 1, r:r + 16, :] + fk[j, s:s + 16, main] * fine_sum(fv1, j, s) + fine_sum(fkv1, j, s)
            ) * finv[j - 1, r:r + 16, :]
            out_ref[j - 1, r:r + 16, :] = (
                (3.0 / 14.0) * fv1[j, s:s + 16, main] - (2.0 / 7.0) * fv[j, s:s + 16, main] + (15.0 / 14.0) * goal
            )
        return carry

    sent(level_in + fine_in + fine_out)
    lax.fori_loop(1, depth + 1, fine_two, 0)


def per_device(sizes, *args):
    fine, level, coarse = args[0], args[3], args[6]
    count_z, count_y, wr, wc = sizes
    depth, rows, cols = fine.shape
    ldepth = level.shape[0]
    i32 = jnp.int32
    planes = ldepth + 6
    big = (depth + 2, rows + 16, cols + 128)
    small = (planes, wr, wc)

    def vmem(shape, dtype=F32):
        return pltpu.VMEM(shape, dtype)

    scratch = [
        vmem(fine.shape), vmem(fine.shape), vmem(fine.shape, i32),
        vmem((2, rows, cols)), vmem((2, rows, cols), i32),
        vmem((depth, rows, 128)), vmem((depth, rows, 128), i32),
        vmem((2, depth, cols)), vmem((2, depth, cols), i32),
        vmem((2, depth, cols)), vmem((2, depth, cols), i32),
        vmem(small), vmem((ldepth + 4, wr, wc)), vmem(small, i32),
        vmem((ldepth // 2 + 4,) + coarse.shape[1:]),
        vmem((ldepth // 2 + 4, coarse.shape[1], wc)),
        vmem(small), vmem(small), vmem(small), vmem(small), vmem(small), vmem(small),
        vmem((wr, cols + 128)), vmem((ldepth + 2, rows + 16, cols + 128)),
        vmem(big), vmem(big), vmem(big), vmem(big), vmem(big), vmem(fine.shape),
        vmem((depth, rows, 128)), vmem((2, depth, cols)), vmem((2, depth, cols)),
        pltpu.SemaphoreType.DMA((7,)),
        pltpu.SemaphoreType.DMA((23,)),
        pltpu.SemaphoreType.DMA((23,)),
    ]
    return pl.pallas_call(
        functools.partial(kernel, sizes),
        out_shape=jax.ShapeDtypeStruct(fine.shape, F32),
        in_specs=[pl.BlockSpec(memory_space=pl.ANY)] * 7 + [pl.BlockSpec(memory_space=pltpu.SMEM)],
        out_specs=pl.BlockSpec(memory_space=pltpu.VMEM),
        scratch_shapes=scratch,
        compiler_params=pltpu.CompilerParams(
            collective_id=0, has_side_effects=True, vmem_limit_bytes=56 * 1024 * 1024
        ),
    )(*args)


def solution(mesh):
    count_z, count_y = mesh.shape["gx"], mesh.shape["gy"]
    sizes = (count_z, count_y, 40 if count_y <= 2 else 48, 384)
    return jax.shard_map(
        functools.partial(per_device, sizes),
        mesh=mesh,
        in_specs=(
            P(("grp", "gx"), "gy", "wa"),
            P(("grp", "gx"), "gy", "wa"),
            P(("grp", "gx"), "gy", "wa"),
            P(("grp", "gx"), None, None),
            P(("grp", "gx"), None, None),
            P(("grp", "gx"), None, None),
            P(("grp", "gx"), None, None),
            P(),
        ),
        out_specs=P(("grp", "gx"), "gy", "wa"),
        check_vma=False,
    )
```

time: 210 us -> 57.6 us (0.27); the launches traced: 207 us -> 57.5 us
  starting transfers between devices: 75.6 us -> 0 us
  other arithmetic: 72.3 us -> 0 us
  Pallas kernels: 0 us -> 54.3 us
  local copies, waits for them, and re-layouts: 30.2 us -> 3.14 us
  waiting for transfers between devices: 19.1 us -> 0 us
  matrix products: 8.99 us -> 0 us
    ppermute x28 -> x0, starting transfers between devices: 75.6 us -> none  [the longest x14 57.2 us: extended(): lax.ppermute(lax.slice_in_dim(block, block.shape[dim] - width, None, axis...]
    pallas_call x0 -> x1, Pallas kernels: none -> 54.3 us  [per_device(): pl.pallas_call(functools.partial(kernel, sizes), out_shape=jax.ShapeDtype...]
    add x5 -> x0, other arithmetic: 48.4 us -> none  [the longest x2 24.5 us: smooth(): return field + step_two]
    ppermute x28 -> x0, waiting for transfers between devices: 19.1 us -> none  [the longest x14 14.5 us: extended(): lax.ppermute(lax.slice_in_dim(block, 0, width, axis=dim), axis, backward)]
    select_n x2 -> x0, other arithmetic: 14 us -> none  [lookup(): kappa = jnp.where(ids == material, table[material], kappa)]
    slice x15 -> x0, local copies, waits for them, and re-layouts: 12.5 us -> none  [the longest x10 7.11 us: extended(): lax.slice_in_dim(block, block.shape[dim] - width, None, axis=dim)]
    ppermute x6 -> x0, local copies, waits for them, and re-layouts: 9.54 us -> none  [the longest x3 4.79 us: extended(): lax.ppermute(lax.slice_in_dim(block, block.shape[dim] - width, None, axis...]
    dot_general x2 -> x0, matrix products: 8.99 us -> none  [prolong(): jnp.dot(flat, matrix, precision=lax.Precision.HIGHEST, preferred_element_...]
  transfers between devices with their start and end apart: 28 -> 0, of which waited for: 10 -> 0; matrix products, arithmetic and copies ran while one was open for 27% -> 0% of each run, Pallas kernels for 0% -> 0%
where the time goes in v1:
time: 57.6 us; the launch traced here: 57.5 us
  Pallas kernels  54.3 us (94%)
  local copies, waits for them, and re-layouts  3.14 us (5%)
    pallas_call x1, Pallas kernels, per_device(): pl.pallas_call(functools.partial(kernel, sizes), out_shape=jax.ShapeDtype...  54.3 us
    unnamed x1, local copies, waits for them, and re-layouts  3.14 us

profile of v1, /device:TPU:0, one launch (start us, length us, event | category | flops | bytes accessed | tf_op | source)
XLA Modules:
  0.0 57.5 jit_solution(6455705772148998667)
XLA Ops:
  0.0 54.3 %shard_map.82 = f32[16,64,512]{2,1,0:T(8,128)} custom-call(f32[16,64,512]{2,1,0:T(8,128)} %fi_hbm.1, f32[16,64,512]{2,1,0:T(8,128)} %fr_hbm.1, s32[16,64,512]{2,1,0:T(8,128)} %fid_hbm.1, f32[8,64,512]{2,1,0:T(8,128)} %li_hbm.1, f32[8,64,512]{2,1,0:T(8,128)} %lr_hbm.1, s32[8,64,512]{2,1,0:T(8,128)} %lid_hbm.1, f32[4,32,256]{2,1,0:T(8,128)} %co_hbm.1, f32[8]{0:T(128)} %table_ref.1), custom_call_target="tpu_custom_call" | custom-call | tf_op jit(solution)/shard_map/pallas_call | solution.py:367
  54.4 3.1 %copy.10 = f32[16,64,512]{2,1,0:T(8,128)} copy(f32[16,64,512]{2,1,0:T(8,128)} %shard_map.82) | data formatting | bytes 4194304

commit v2 on v1

--- a/solution.py
+++ b/solution.py
@@ -8,7 +8,7 @@
 from jax.sharding import PartitionSpec as P
 
 F32 = jnp.float32
-HI = lax.Precision.HIGHEST
+BF16 = jnp.bfloat16
 
 
 def lookup(ids, table):
@@ -31,6 +31,15 @@
     return jnp.where((fine >= 0) & (fine < total), both, 0.0).astype(F32)
 
 
+def halves(field, axis):
+    high = field.astype(BF16).astype(F32)
+    return jnp.concatenate([high, field - high], axis=axis).astype(BF16)
+
+
+def twice(weights, axis):
+    return jnp.concatenate([weights, weights], axis=axis).astype(BF16)
+
+
 def inverse(kappa, around):
     return jnp.where(kappa > 0.0, 1.0 / (6.0 * kappa + around), 0.0)
 
@@ -41,7 +50,7 @@
     out_ref,
     fi, fr, fid, fiz, fidz, fix, fidx, ysend, yidsend, yrecv, yidrecv,
     li, lr, lid, co, xc,
-    lk, lv, lkv, lv1, lkv1, linv, mid, pm,
+    lk, lv, lkv, lv1, lkv1, linv, mid, wide, pm,
     fk, fv, fkv, fv1, fkv1, finv, vx, vysend, vyrecv,
     local_sem, send_sem, recv_sem,
 ):
@@ -120,8 +129,8 @@
             send(src.at[(pl.ds(0, width),) + win], dst.at[pl.ds(own + count, width)], zm, has_zm, has_zp),
         ]
 
-    level_in = z_pair(co_hbm, co, 2, 2)
-    level_in += z_pair(li_hbm, li, 3, 3)
+    coarse_in = z_pair(co_hbm, co, 2, 2)
+    level_in = z_pair(li_hbm, li, 3, 3)
     level_in += z_pair(lid_hbm, lid, 3, 3)
     level_in += z_pair(lr_hbm, lr, 2, 2)
     edge0 = pl.multiple_of((1 - wa) * (cols - 128), 128)
@@ -129,9 +138,6 @@
         send(fid_hbm.at[:, :, pl.ds(edge0, 128)], fidx, other, None, None),
         send(fi_hbm.at[:, :, pl.ds(edge0, 128)], fix, other, None, None),
     ]
-    for src, dst in ((fid_hbm, fidz), (fi_hbm, fiz)):
-        fine_in.append(send(src.at[pl.ds(depth - 1, 1)], dst.at[pl.ds(0, 1)], zp, has_zp, has_zm))
-        fine_in.append(send(src.at[pl.ds(0, 1)], dst.at[pl.ds(1, 1)], zm, has_zm, has_zp))
     local[4].wait()
     local[5].wait()
     for src, pack, dst in ((fid, yidsend, yidrecv), (fi, ysend, yrecv)):
@@ -142,23 +148,33 @@
         fine_in.append(send(pack.at[1], dst.at[1], ym, has_ym, has_yp))
 
     table = [table_ref[m] for m in range(table_ref.shape[0])]
-    mx = weights_of((ccols, wc), 1, col0, lcols, 0)
-    my = weights_of((wr, crows), 0, row0, lrows, 0)
-    mx2 = weights_of((wc, cols + 128), 1, wa * cols, 2 * lcols, col0, (cols + 64, cols + 128))
-    my2 = weights_of((rows + 16, wr), 0, gy * rows - 8, 2 * lrows, row0)
+    main = slice(0, cols)
+    rim = slice(cols, cols + 128)
+
+    def fine_kappa(j, carry):
+        for r in range(0, rows, 16):
+            fk[j, 8 + r:24 + r, main] = lookup(fid[j - 1, r:r + 16, :], table)
+        return carry
+
+    lax.fori_loop(1, depth + 1, fine_kappa, 0)
+
+    mx = twice(weights_of((ccols, wc), 1, col0, lcols, 0), 0)
+    my = twice(weights_of((wr, crows), 0, row0, lrows, 0), 1)
+    mx2 = twice(weights_of((wc, cols + 128), 1, wa * cols, 2 * lcols, col0, (cols + 64, cols + 128)), 0)
+    my2 = twice(weights_of((rows + 16, wr), 0, gy * rows - 8, 2 * lrows, row0), 1)
 
     for copy in local[:4]:
         copy.wait()
-    receive(level_in)
+    receive(coarse_in)
 
     planes = ldepth + 6
-    for p in range(ldepth // 2 + 4):
-        field = co[p]
-        if p < 2:
-            field = jnp.where(has_zm, field, 0.0)
-        if p >= ldepth // 2 + 2:
-            field = jnp.where(has_zp, field, 0.0)
-        xc[p] = jnp.dot(field, mx, precision=HI, preferred_element_type=F32)
+    cplanes = ldepth // 2 + 4
+    coarse = jnp.concatenate(
+        [jnp.where(has_zm, co[0:2], 0.0), co[2:cplanes - 2], jnp.where(has_zp, co[cplanes - 2:], 0.0)], axis=0
+    )
+    xc[...] = jnp.dot(
+        halves(coarse.reshape(cplanes * crows, ccols), 1), mx, preferred_element_type=F32
+    ).reshape(cplanes, crows, wc)
     lrow = lax.broadcasted_iota(jnp.int32, (wr, wc), 0)
     lcol = lax.broadcasted_iota(jnp.int32, (wr, wc), 1)
     inside = (lrow != jnp.where(gy == 0, wr - 1, 0)) & (lcol != jnp.where(wa == 0, wc - 1, 0))
@@ -166,7 +182,7 @@
     def level_start(p, carry):
         base = (p + 1) // 2
         side = base + 2 * ((p + 1) % 2) - 1
-        spread = jnp.dot(my, 0.75 * xc[base] + 0.25 * xc[side], precision=HI, preferred_element_type=F32)
+        spread = jnp.dot(my, halves(0.75 * xc[base] + 0.25 * xc[side], 0), preferred_element_type=F32)
         here = ((p >= 3) | has_zm) & ((p < ldepth + 3) | has_zp)
         keep = inside & here
         kappa = jnp.where(keep, lookup(lid[p], table), 0.0)
@@ -175,8 +191,6 @@
         lv[p] = field
         lkv[p] = kappa * field
         return carry
-
-    lax.fori_loop(0, planes, level_start, 0)
 
     def level_sum(ref, p):
         field = ref[p]
@@ -198,18 +212,40 @@
         lkv1[p] = kappa * new
         return carry
 
-    lax.fori_loop(1, planes - 1, level_one, 0)
-
     def level_two(p, carry):
         inv = linv[p]
         rhs = jnp.where(inv > 0.0, lr[p - 1], 0.0)
         goal = (2.0 * rhs + lk[p] * level_sum(lv1, p) + level_sum(lkv1, p)) * inv
-        settled = (3.0 / 14.0) * lv1[p] - (2.0 / 7.0) * lv[p] + (15.0 / 14.0) * goal
-        mid[...] = jnp.dot(settled, mx2, precision=HI, preferred_element_type=F32)
-        pm[p - 2] = jnp.dot(my2, mid[...], precision=HI, preferred_element_type=F32)
-        return carry
-
-    lax.fori_loop(2, planes - 2, level_two, 0)
+        mid[p - 2] = (3.0 / 14.0) * lv1[p] - (2.0 / 7.0) * lv[p] + (15.0 / 14.0) * goal
+        return carry
+
+    def spread_rows(p, carry):
+        pm[p - 2] = jnp.dot(my2, halves(wide[p - 2], 0), preferred_element_type=F32)
+        return carry
+
+    def level_finish(low, high):
+        lax.fori_loop(low, high, level_two, 0)
+        part = mid[low - 2:high - 2].reshape((high - low) * wr, wc)
+        wide[low - 2:high - 2] = jnp.dot(
+            halves(part, 1), mx2, preferred_element_type=F32
+        ).reshape(high - low, wr, cols + 128)
+        lax.fori_loop(low, high, spread_rows, 0)
+
+    lax.fori_loop(3, planes - 3, level_start, 0)
+    lax.fori_loop(4, planes - 4, level_one, 0)
+    level_finish(5, planes - 5)
+
+    receive(level_in)
+    for src, dst in ((fid_hbm, fidz), (fi_hbm, fiz)):
+        fine_in.append(send(src.at[pl.ds(depth - 1, 1)], dst.at[pl.ds(0, 1)], zp, has_zp, has_zm))
+        fine_in.append(send(src.at[pl.ds(0, 1)], dst.at[pl.ds(1, 1)], zm, has_zm, has_zp))
+
+    lax.fori_loop(0, 3, level_start, 0)
+    lax.fori_loop(planes - 3, planes, level_start, 0)
+    lax.fori_loop(1, 4, level_one, 0)
+    lax.fori_loop(planes - 4, planes - 1, level_one, 0)
+    level_finish(2, 5)
+    level_finish(planes - 5, planes - 2)
 
     local[6].wait()
     receive(fine_in)
@@ -221,9 +257,6 @@
         base = (j + 1) // 2
         side = base + 2 * ((j + 1) % 2) - 1
         return 0.75 * pm[(base,) + where + (width,)] + 0.25 * pm[(side,) + where + (width,)]
-
-    main = slice(0, cols)
-    rim = slice(cols, cols + 128)
 
     def put(j, where, width, kappa, field):
         fk[(j,) + where + (width,)] = kappa
@@ -242,11 +275,9 @@
     def fine_start(j, carry):
         for r in range(0, rows, 16):
             at = (pl.ds(8 + r, 16),)
-            put(
-                j, at, main,
-                lookup(fid[j - 1, r:r + 16, :], table),
-                fi[j - 1, r:r + 16, :] + spread_at(j, at, main),
-            )
+            field = fi[j - 1, r:r + 16, :] + spread_at(j, at, main)
+            fv[j, 8 + r:24 + r, main] = field
+            fkv[j, 8 + r:24 + r, main] = fk[j, 8 + r:24 + r, main] * field
             put(
                 j, at, rim,
                 jnp.where(edge_in, lookup(fidx[j - 1, r:r + 16, :], table), 0.0),
@@ -282,28 +313,30 @@
             new = field + (goal - field) * (1.0 / 1.2)
             fv1[j, s:s + 16, main] = new
             fkv1[j, s:s + 16, main] = kappa * new
-        return carry
-
-    lax.fori_loop(1, depth + 1, fine_one, 0)
+        for n, row in ((0, rows + 7), (1, 8)):
+            vysend[n, pl.ds(j - 1, 1), :] = fv1[j, pl.ds(row, 1), main]
+        return carry
 
     own = pl.ds(8, rows)
-    fine_out = [
+
+    def rim_sends(first, count):
+        group = pl.ds(first, count)
+        return [
+            send(fv1.at[pl.ds(first + 1, count), own, pl.ds(edge0, 128)], vx.at[group], other, None, None),
+            send(vysend.at[0, group], vyrecv.at[0, group], yp, has_yp, has_ym),
+            send(vysend.at[1, group], vyrecv.at[1, group], ym, has_ym, has_yp),
+        ]
+
+    half = depth // 2
+    lax.fori_loop(0, 2, lambda i, carry: fine_one(1 + i * (depth - 1), carry), 0)
+    faces = [
         send(fv1.at[pl.ds(depth, 1), own, pl.ds(0, cols)], fv1.at[pl.ds(0, 1), own, pl.ds(0, cols)], zp, has_zp, has_zm),
         send(fv1.at[pl.ds(1, 1), own, pl.ds(0, cols)], fv1.at[pl.ds(depth + 1, 1), own, pl.ds(0, cols)], zm, has_zm, has_zp),
-        send(fv1.at[pl.ds(1, depth), own, pl.ds(edge0, 128)], vx, other, None, None),
     ]
-    for z in range(depth):
-        vysend[0, pl.ds(z, 1), :] = fv1[z + 1, pl.ds(rows + 7, 1), main]
-        vysend[1, pl.ds(z, 1), :] = fv1[z + 1, pl.ds(8, 1), main]
-    fine_out.append(send(vysend.at[0], vyrecv.at[0], yp, has_yp, has_ym))
-    fine_out.append(send(vysend.at[1], vyrecv.at[1], ym, has_ym, has_yp))
-    receive(fine_out)
-
-    for j, there in ((0, has_zm), (depth + 1, has_zp)):
-        for r in range(8, rows + 8, 16):
-            field = jnp.where(there, fv1[j, r:r + 16, main], 0.0)
-            fv1[j, r:r + 16, main] = field
-            fkv1[j, r:r + 16, main] = fk[j, r:r + 16, main] * field
+    lax.fori_loop(2, half + 1, fine_one, 0)
+    rims_low = rim_sends(0, half)
+    lax.fori_loop(half + 1, depth, fine_one, 0)
+    rims_high = rim_sends(half, depth - half)
 
     def fine_rims(j, carry):
         for r in range(0, rows, 16):
@@ -317,9 +350,8 @@
             fkv1[j, pl.ds(row, 1), main] = fk[j, pl.ds(row, 1), main] * field
         return carry
 
-    lax.fori_loop(1, depth + 1, fine_rims, 0)
-
     def fine_two(j, carry):
+        fine_rims(j, 0)
         for r in range(0, rows, 16):
             s = 8 + r
             goal = (
@@ -330,8 +362,18 @@
             )
         return carry
 
-    sent(level_in + fine_in + fine_out)
-    lax.fori_loop(1, depth + 1, fine_two, 0)
+    receive(rims_low)
+    receive(faces)
+    sent(faces)
+    for j, there in ((0, has_zm), (depth + 1, has_zp)):
+        for r in range(8, rows + 8, 16):
+            field = jnp.where(there, fv1[j, r:r + 16, main], 0.0)
+            fv1[j, r:r + 16, main] = field
+            fkv1[j, r:r + 16, main] = fk[j, r:r + 16, main] * field
+    lax.fori_loop(1, half + 1, fine_two, 0)
+    receive(rims_high)
+    lax.fori_loop(half + 1, depth + 1, fine_two, 0)
+    sent(coarse_in + level_in + fine_in + rims_low + rims_high)
 
 
 def per_device(sizes, *args):
@@ -357,12 +399,12 @@
         vmem((ldepth // 2 + 4,) + coarse.shape[1:]),
         vmem((ldepth // 2 + 4, coarse.shape[1], wc)),
         vmem(small), vmem(small), vmem(small), vmem(small), vmem(small), vmem(small),
-        vmem((wr, cols + 128)), vmem((ldepth + 2, rows + 16, cols + 128)),
+        vmem((ldepth + 2, wr, wc)), vmem((ldepth + 2, wr, cols + 128)), vmem((ldepth + 2, rows + 16, cols + 128)),
         vmem(big), vmem(big), vmem(big), vmem(big), vmem(big), vmem(fine.shape),
         vmem((depth, rows, 128)), vmem((2, depth, cols)), vmem((2, depth, cols)),
         pltpu.SemaphoreType.DMA((7,)),
-        pltpu.SemaphoreType.DMA((23,)),
-        pltpu.SemaphoreType.DMA((23,)),
+        pltpu.SemaphoreType.DMA((26,)),
+        pltpu.SemaphoreType.DMA((26,)),
     ]
     return pl.pallas_call(
         functools.partial(kernel, sizes),

time: 57.6 us -> 42.6 us (0.74)
  Pallas kernels: 54.3 us -> 39.3 us
    pallas_call x1, Pallas kernels: 54.3 us -> 39.3 us  [per_device(): pl.pallas_call(functools.partial(kernel, sizes), out_shape=jax.ShapeDtype...]
where the time goes in v2:
time: 42.6 us; the launch traced here: 42.4 us
  Pallas kernels  39.3 us (92%)
  local copies, waits for them, and re-layouts  3.14 us (7%)
    pallas_call x1, Pallas kernels, per_device(): pl.pallas_call(functools.partial(kernel, sizes), out_shape=jax.ShapeDtype...  39.3 us
    unnamed x1, local copies, waits for them, and re-layouts  3.14 us

profile of v2, /device:TPU:0, one launch (start us, length us, event | category | flops | bytes accessed | tf_op | source)
XLA Modules:
  0.0 42.4 jit_solution(4762340958330675361)
XLA Ops:
  0.0 39.3 %shard_map.82 = f32[16,64,512]{2,1,0:T(8,128)} custom-call(f32[16,64,512]{2,1,0:T(8,128)} %fi_hbm.1, f32[16,64,512]{2,1,0:T(8,128)} %fr_hbm.1, s32[16,64,512]{2,1,0:T(8,128)} %fid_hbm.1, f32[8,64,512]{2,1,0:T(8,128)} %li_hbm.1, f32[8,64,512]{2,1,0:T(8,128)} %lr_hbm.1, s32[8,64,512]{2,1,0:T(8,128)} %lid_hbm.1, f32[4,32,256]{2,1,0:T(8,128)} %co_hbm.1, f32[8]{0:T(128)} %table_ref.1), custom_call_target="tpu_custom_call" | custom-call | tf_op jit(solution)/shard_map/pallas_call | solution.py:409
  39.3 3.1 %copy.10 = f32[16,64,512]{2,1,0:T(8,128)} copy(f32[16,64,512]{2,1,0:T(8,128)} %shard_map.82) | data formatting | bytes 4194304

commit v3 on v2

--- a/solution.py
+++ b/solution.py
@@ -123,11 +123,32 @@
 
     def z_pair(src, dst, width, own):
         count = src.shape[0]
-        win = (pl.ds(row0, wr), pl.ds(col0, wc)) if dst.shape[1] == wr else (slice(None), slice(None))
+        lanes = src.shape[2] // 2
+        window = dst.shape[1] == wr
+        height = pl.ds(row0, wr) if window else slice(None)
+        src0 = pl.multiple_of(wa * lanes, 128)
+        dst0 = pl.multiple_of(wa * (dst.shape[2] - lanes), 128)
+        take, place = pl.ds(src0, lanes), pl.ds(dst0, lanes)
         return [
-            send(src.at[(pl.ds(count - width, width),) + win], dst.at[pl.ds(own - width, width)], zp, has_zp, has_zm),
-            send(src.at[(pl.ds(0, width),) + win], dst.at[pl.ds(own + count, width)], zm, has_zm, has_zp),
+            send(src.at[pl.ds(count - width, width), height, take], dst.at[pl.ds(own - width, width), :, place], zp, has_zp, has_zm),
+            send(src.at[pl.ds(0, width), height, take], dst.at[pl.ds(own + count, width), :, place], zm, has_zm, has_zp),
         ]
+
+    def forward(pair, src, dst, width, own):
+        window = dst.shape[1] == wr
+        lanes = src.shape[2] // 2
+        from0 = pl.multiple_of(jnp.where(wa == 0, lanes - 128, dst.shape[2] - lanes) if window else wa * lanes, 128)
+        to0 = pl.multiple_of(wa * (dst.shape[2] - 128) if window else wa * lanes, 128)
+        width_lanes = 128 if window else lanes
+        result = []
+        for copy, first, there in ((pair[0], own - width, has_zm), (pair[1], own + src.shape[0], has_zp)):
+            receive([copy])
+            layers = pl.ds(first, width)
+            result.append(send(
+                dst.at[layers, :, pl.ds(from0, width_lanes)], dst.at[layers, :, pl.ds(to0, width_lanes)],
+                other, there, there,
+            ))
+        return result
 
     coarse_in = z_pair(co_hbm, co, 2, 2)
     level_in = z_pair(li_hbm, li, 3, 3)
@@ -158,6 +179,7 @@
 
     lax.fori_loop(1, depth + 1, fine_kappa, 0)
 
+    coarse_more = forward(coarse_in, co_hbm, co, 2, 2)
     mx = twice(weights_of((ccols, wc), 1, col0, lcols, 0), 0)
     my = twice(weights_of((wr, crows), 0, row0, lrows, 0), 1)
     mx2 = twice(weights_of((wc, cols + 128), 1, wa * cols, 2 * lcols, col0, (cols + 64, cols + 128)), 0)
@@ -165,7 +187,7 @@
 
     for copy in local[:4]:
         copy.wait()
-    receive(coarse_in)
+    receive(coarse_more)
 
     planes = ldepth + 6
     cplanes = ldepth // 2 + 4
@@ -235,11 +257,14 @@
     lax.fori_loop(4, planes - 4, level_one, 0)
     level_finish(5, planes - 5)
 
-    receive(level_in)
+    level_more = forward(level_in[0:2], li_hbm, li, 3, 3)
+    level_more += forward(level_in[2:4], lid_hbm, lid, 3, 3)
+    level_more += forward(level_in[4:6], lr_hbm, lr, 2, 2)
     for src, dst in ((fid_hbm, fidz), (fi_hbm, fiz)):
         fine_in.append(send(src.at[pl.ds(depth - 1, 1)], dst.at[pl.ds(0, 1)], zp, has_zp, has_zm))
         fine_in.append(send(src.at[pl.ds(0, 1)], dst.at[pl.ds(1, 1)], zm, has_zm, has_zp))
 
+    receive(level_more)
     lax.fori_loop(0, 3, level_start, 0)
     lax.fori_loop(planes - 3, planes, level_start, 0)
     lax.fori_loop(1, 4, level_one, 0)
@@ -373,7 +398,7 @@
     lax.fori_loop(1, half + 1, fine_two, 0)
     receive(rims_high)
     lax.fori_loop(half + 1, depth + 1, fine_two, 0)
-    sent(coarse_in + level_in + fine_in + rims_low + rims_high)
+    sent(coarse_in + coarse_more + level_in + level_more + fine_in + rims_low + rims_high)
 
 
 def per_device(sizes, *args):
@@ -403,13 +428,13 @@
         vmem(big), vmem(big), vmem(big), vmem(big), vmem(big), vmem(fine.shape),
         vmem((depth, rows, 128)), vmem((2, depth, cols)), vmem((2, depth, cols)),
         pltpu.SemaphoreType.DMA((7,)),
-        pltpu.SemaphoreType.DMA((26,)),
-        pltpu.SemaphoreType.DMA((26,)),
+        pltpu.SemaphoreType.DMA((34,)),
+        pltpu.SemaphoreType.DMA((34,)),
     ]
     return pl.pallas_call(
         functools.partial(kernel, sizes),
-        out_shape=jax.ShapeDtypeStruct(fine.shape, F32),
-        in_specs=[pl.BlockSpec(memory_space=pl.ANY)] * 7 + [pl.BlockSpec(memory_space=pltpu.SMEM)],
+        out_shape=pltpu.VMEM(fine.shape, F32),
+        in_specs=[pl.BlockSpec(memory_space=pltpu.HBM)] * 7 + [pl.BlockSpec(memory_space=pltpu.SMEM)],
         out_specs=pl.BlockSpec(memory_space=pltpu.VMEM),
         scratch_shapes=scratch,
         compiler_params=pltpu.CompilerParams(

time: 42.6 us -> 36.1 us (0.85)
  Pallas kernels: 39.3 us -> 34.6 us
  local copies, waits for them, and re-layouts: 3.14 us -> 1.32 us
    pallas_call x1, Pallas kernels: 39.3 us -> 34.6 us  [per_device(): pl.pallas_call(functools.partial(kernel, sizes), out_shape=pltpu.VMEM(fin...]
    unnamed x1, local copies, waits for them, and re-layouts: 3.14 us -> 1.32 us
where the time goes in v3:
time: 36.1 us; the launch traced here: 35.9 us
  Pallas kernels  34.6 us (96%)
  local copies, waits for them, and re-layouts  1.32 us (4%)
    pallas_call x1, Pallas kernels, per_device(): pl.pallas_call(functools.partial(kernel, sizes), out_shape=pltpu.VMEM(fin...  34.6 us
    unnamed x1, local copies, waits for them, and re-layouts  1.32 us

profile of v3, /device:TPU:0, one launch (start us, length us, event | category | flops | bytes accessed | tf_op | source)
XLA Modules:
  0.0 35.9 jit_solution(14827204663657213042)
XLA Ops:
  0.0 34.6 %shard_map.82 = f32[16,64,512]{2,1,0:T(8,128)S(1)} custom-call(f32[16,64,512]{2,1,0:T(8,128)} %fi_hbm.1, f32[16,64,512]{2,1,0:T(8,128)} %fr_hbm.1, s32[16,64,512]{2,1,0:T(8,128)} %fid_hbm.1, f32[8,64,512]{2,1,0:T(8,128)} %li_hbm.1, f32[8,64,512]{2,1,0:T(8,128)} %lr_hbm.1, s32[8,64,512]{2,1,0:T(8,128)} %lid_hbm.1, f32[4,32,256]{2,1,0:T(8,128)} %co_hbm.1, ...), custom_call_target="tpu_custom_call" | custom-call | tf_op jit(solution)/shard_map/pallas_call | solution.py:434
  34.6 1.3 %copy.10 = f32[16,64,512]{2,1,0:T(8,128)} copy(f32[16,64,512]{2,1,0:T(8,128)S(1)} %shard_map.82) | data formatting | bytes 4194304

commit v4 on v3

--- a/solution.py
+++ b/solution.py
@@ -273,7 +273,7 @@
     level_finish(planes - 5, planes - 2)
 
     local[6].wait()
-    receive(fine_in)
+    receive(fine_in[:6])
     lanes = lax.broadcasted_iota(jnp.int32, (16, 128), 1)
     edge_in = jnp.where(wa == 0, 0, 64)
     edge_in = (lanes >= edge_in) & (lanes < edge_in + 64)
@@ -287,15 +287,6 @@
         fk[(j,) + where + (width,)] = kappa
         fv[(j,) + where + (width,)] = field
         fkv[(j,) + where + (width,)] = kappa * field
-
-    for n, j, there in ((0, 0, has_zm), (1, depth + 1, has_zp)):
-        for r in range(0, rows, 16):
-            at = (pl.ds(8 + r, 16),)
-            put(
-                j, at, main,
-                jnp.where(there, lookup(fidz[n, r:r + 16, :], table), 0.0),
-                jnp.where(there, fiz[n, r:r + 16, :] + spread_at(j, at, main), 0.0),
-            )
 
     def fine_start(j, carry):
         for r in range(0, rows, 16):
@@ -353,12 +344,22 @@
         ]
 
     half = depth // 2
+    lax.fori_loop(2, half + 1, fine_one, 0)
+    receive(fine_in[6:])
+    for n, j, there in ((0, 0, has_zm), (1, depth + 1, has_zp)):
+        for r in range(0, rows, 16):
+            at = (pl.ds(8 + r, 16),)
+            put(
+                j, at, main,
+                jnp.where(there, lookup(fidz[n, r:r + 16, :], table), 0.0),
+                jnp.where(there, fiz[n, r:r + 16, :] + spread_at(j, at, main), 0.0),
+            )
+
     lax.fori_loop(0, 2, lambda i, carry: fine_one(1 + i * (depth - 1), carry), 0)
     faces = [
         send(fv1.at[pl.ds(depth, 1), own, pl.ds(0, cols)], fv1.at[pl.ds(0, 1), own, pl.ds(0, cols)], zp, has_zp, has_zm),
         send(fv1.at[pl.ds(1, 1), own, pl.ds(0, cols)], fv1.at[pl.ds(depth + 1, 1), own, pl.ds(0, cols)], zm, has_zm, has_zp),
     ]
-    lax.fori_loop(2, half + 1, fine_one, 0)
     rims_low = rim_sends(0, half)
     lax.fori_loop(half + 1, depth, fine_one, 0)
     rims_high = rim_sends(half, depth - half)
@@ -388,6 +389,9 @@
         return carry
 
     receive(rims_low)
+    lax.fori_loop(2, half + 1, fine_two, 0)
+    receive(rims_high)
+    lax.fori_loop(half + 1, depth, fine_two, 0)
     receive(faces)
     sent(faces)
     for j, there in ((0, has_zm), (depth + 1, has_zp)):
@@ -395,9 +399,7 @@
             field = jnp.where(there, fv1[j, r:r + 16, main], 0.0)
             fv1[j, r:r + 16, main] = field
             fkv1[j, r:r + 16, main] = fk[j, r:r + 16, main] * field
-    lax.fori_loop(1, half + 1, fine_two, 0)
-    receive(rims_high)
-    lax.fori_loop(half + 1, depth + 1, fine_two, 0)
+    lax.fori_loop(0, 2, lambda i, carry: fine_two(1 + i * (depth - 1), carry), 0)
     sent(coarse_in + coarse_more + level_in + level_more + fine_in + rims_low + rims_high)
 
 

time: 36.1 us -> 33.9 us (0.939)
  Pallas kernels: 34.6 us -> 32.4 us
    pallas_call x1, Pallas kernels: 34.6 us -> 32.4 us  [per_device(): pl.pallas_call(functools.partial(kernel, sizes), out_shape=pltpu.VMEM(fin...]
where the time goes in v4:
time: 33.9 us; the launch traced here: 33.7 us
  Pallas kernels  32.4 us (96%)
  local copies, waits for them, and re-layouts  1.32 us (4%)
    pallas_call x1, Pallas kernels, per_device(): pl.pallas_call(functools.partial(kernel, sizes), out_shape=pltpu.VMEM(fin...  32.4 us
    unnamed x1, local copies, waits for them, and re-layouts  1.32 us

profile of v4, /device:TPU:0, one launch (start us, length us, event | category | flops | bytes accessed | tf_op | source)
XLA Modules:
  0.0 33.7 jit_solution(4713238069825369365)
XLA Ops:
  0.0 32.4 %shard_map.82 = f32[16,64,512]{2,1,0:T(8,128)S(1)} custom-call(f32[16,64,512]{2,1,0:T(8,128)} %fi_hbm.1, f32[16,64,512]{2,1,0:T(8,128)} %fr_hbm.1, s32[16,64,512]{2,1,0:T(8,128)} %fid_hbm.1, f32[8,64,512]{2,1,0:T(8,128)} %li_hbm.1, f32[8,64,512]{2,1,0:T(8,128)} %lr_hbm.1, s32[8,64,512]{2,1,0:T(8,128)} %lid_hbm.1, f32[4,32,256]{2,1,0:T(8,128)} %co_hbm.1, ...), custom_call_target="tpu_custom_call" | custom-call | tf_op jit(solution)/shard_map/pallas_call | solution.py:436
  32.4 1.3 %copy.10 = f32[16,64,512]{2,1,0:T(8,128)} copy(f32[16,64,512]{2,1,0:T(8,128)S(1)} %shard_map.82) | data formatting | bytes 4194304
